TPU v7x, 128 devices: a whole 4x4x4 slice. The times are simulated.
128 devices in a mesh: dp: 16 (over y_hi, z, core), mp: 8 (over y_lo, x).
Axes of the slice: x: 4, y: 4 (y_hi: 2, y_lo: 2; y = y_hi * 2 + y_lo), z: 4, core: 2. Of those that a mesh axis runs over, the one named last changes fastest.
Arguments:
- latents: bfloat16 [32, 512, 1024], P('dp', 'mp'), may hold values from -6 to 6
- pixels: bfloat16 [32, 4096, 261], P('dp', 'mp'), may hold values from -6 to 6
- masks: int32 [32, 4096], P('dp', 'mp'), may hold values from 0 to 1, as said below
- cotangent: bfloat16 [32, 512, 1024], P('dp', 'mp'), may hold values from -6 to 6
- norm_latent: float32 [1024], replicated, may hold values from 0.5 to 1.5
- norm_pixel: float32 [261], replicated, may hold values from 0.5 to 1.5
- norm_feed: float32 [1024], replicated, may hold values from 0.5 to 1.5
- norm_self: float32 [1024], replicated, may hold values from 0.5 to 1.5
- norm_last: float32 [1024], replicated, may hold values from 0.5 to 1.5
- cross_query: bfloat16 [1024, 1024], P(None, 'mp'), may hold values from -0.1875 to 0.1875
- cross_key: bfloat16 [261, 1024], P(None, 'mp'), may hold values from -0.375 to 0.375
- cross_value: bfloat16 [261, 1024], P(None, 'mp'), may hold values from -0.375 to 0.375
- cross_out: bfloat16 [1024, 1024], P(None, 'mp'), may hold values from -0.75 to 0.75
- feed_in: bfloat16 [1024, 1024], P(None, 'mp'), may hold values from -0.1875 to 0.1875
- feed_out: bfloat16 [1024, 1024], P('mp'), may hold values from -0.1875 to 0.1875
- self_query: bfloat16 [1024, 1024], P(None, 'mp'), may hold values from -0.1875 to 0.1875
- self_key: bfloat16 [1024, 1024], P(None, 'mp'), may hold values from -0.1875 to 0.1875
- self_value: bfloat16 [1024, 1024], P(None, 'mp'), may hold values from -0.1875 to 0.1875
- self_out: bfloat16 [1024, 1024], P('mp'), may hold values from -0.75 to 0.75
- last_in: bfloat16 [1024, 1024], P(None, 'mp'), may hold values from -0.1875 to 0.1875
- last_out: bfloat16 [1024, 1024], P('mp'), may hold values from -0.1875 to 0.1875
Outputs:
- result: bfloat16 [32, 512, 1024], P('dp', 'mp')
- grad_latents: float32 [32, 512, 1024], P('dp', 'mp')
- grad_pixels: float32 [32, 4096, 261], P('dp', 'mp')
- grad_norm_latent: float32 [1024], replicated
- grad_norm_pixel: float32 [261], replicated
- grad_norm_feed: float32 [1024], replicated
- grad_norm_self: float32 [1024], replicated
- grad_norm_last: float32 [1024], replicated
- grad_cross_query: float32 [1024, 1024], P(None, 'mp')
- grad_cross_key: float32 [261, 1024], P(None, 'mp')
- grad_cross_value: float32 [261, 1024], P(None, 'mp')
- grad_cross_out: float32 [1024, 1024], P(None, 'mp')
- grad_feed_in: float32 [1024, 1024], P(None, 'mp')
- grad_feed_out: float32 [1024, 1024], P('mp')
- grad_self_query: float32 [1024, 1024], P(None, 'mp')
- grad_self_key: float32 [1024, 1024], P(None, 'mp')
- grad_self_value: float32 [1024, 1024], P(None, 'mp')
- grad_self_out: float32 [1024, 1024], P('mp')
- grad_last_in: float32 [1024, 1024], P(None, 'mp')
- grad_last_out: float32 [1024, 1024], P('mp')
Inputs may be any that keep to these rules, and one draw needn't show every extreme that they name: `masks`: each item's kept slots form one rectangle of its 64 x 64 window (slot = row * 64 + column), both sides at least 32; some item keeps the full height of the window and some item exactly (32) squared slots.
All inputs are finite; a program needn't handle non-finite values.
Results may differ from a plain program's by a relative error of at most 0.035.
Values may be sent and summed in bfloat16 or wider, within the bound.
No kernel may reach another device: no remote copies, remote signals or barrier semaphores. Data moves between devices by JAX's collectives and lax.ppermute only.
A program may use at most 128 MiB of HBM per device.

v0:
```python
import jax
import jax.numpy as jnp
from jax import lax
from jax.sharding import PartitionSpec as P

D = 1024
HEADS = 8


epsilon = 1e-05
masked_score = -1e30


def merged(part, axis, combine):
    gathered = jax.tree.map(lambda a: lax.all_gather(a, axis), part)

    def take(source):
        return jax.tree.map(lambda a: lax.dynamic_index_in_dim(a, source, 0, False), gathered)

    return lax.fori_loop(
        1, lax.axis_size(axis), lambda source, state: combine(state, take(source)), take(0)
    )


def layer_norm(values, norm_gain):
    center = values - jnp.mean(values, axis=-1, keepdims=True)
    spread = jnp.mean(center * center, axis=-1, keepdims=True)
    return center * lax.rsqrt(spread + epsilon) * norm_gain


def norm_back(values, norm_gain, upstream):
    unused, pullback = jax.vjp(layer_norm, values, norm_gain)
    return pullback(upstream)


def product(pattern, left_side, right_side):
    return jnp.einsum(pattern, left_side, right_side, preferred_element_type=jnp.float32)


def gather_rows(pieces):
    return lax.all_gather(pieces, "mp", axis=1, tiled=True)


def scatter_rows(partials):
    return lax.psum_scatter(
        partials.astype(jnp.bfloat16), "mp", scatter_dimension=1, tiled=True
    ).astype(jnp.float32)


def gather_grads(pieces):
    return lax.all_gather(pieces, "mp", axis=1, tiled=True)


def scatter_grads(partials):
    return lax.psum_scatter(
        partials.astype(jnp.bfloat16), "mp", scatter_dimension=1, tiled=True
    ).astype(jnp.float32)


def combine_stats(earlier, later):
    peak_score = jnp.maximum(earlier[0], later[0])
    return (
        peak_score,
        earlier[1] * jnp.exp(earlier[0] - peak_score) + later[1] * jnp.exp(later[0] - peak_score),
    )


def feed_forward(stream, norm_gain, weight_in, weight_out):
    hidden = gather_rows(layer_norm(stream, norm_gain).astype(jnp.bfloat16))
    before = product("ild,df->ilf", hidden, weight_in)
    active = jax.nn.gelu(before).astype(jnp.bfloat16)
    return (scatter_rows(product("ilf,fd->ild", active, weight_out)), (hidden, before, active))


def feed_back(stream, norm_gain, weight_in, weight_out, saved, upstream):
    hidden, before, active = saved
    grad_all = gather_grads(upstream.astype(jnp.bfloat16))
    grad_active = product("ild,fd->ilf", grad_all, weight_out)
    grad_wout = product("ilf,ild->fd", active, grad_all)
    unused, gelu_pull = jax.vjp(jax.nn.gelu, before)
    grad_before = gelu_pull(grad_active)[0].astype(jnp.bfloat16)
    grad_win = product("ild,ilf->df", hidden, grad_before)
    grad_hidden = scatter_grads(product("ilf,df->ild", grad_before, weight_in))
    grad_stream, grad_gain = norm_back(stream, norm_gain, grad_hidden)
    return (upstream + grad_stream, grad_gain, grad_win, grad_wout)


def self_forward(stream, norm_gain, weight_query, weight_key, weight_value, weight_out):
    hidden = gather_rows(layer_norm(stream, norm_gain).astype(jnp.bfloat16))
    item_count, row_count = (hidden.shape[0], hidden.shape[1])
    head_width = D // HEADS
    local_heads = weight_query.shape[1] // head_width

    def split_heads(weight):
        return (
            product("ild,de->ile", hidden, weight)
            .astype(jnp.bfloat16)
            .reshape(item_count, row_count, local_heads, head_width)
        )

    queries = split_heads(weight_query)
    key_rows = split_heads(weight_key)
    values = split_heads(weight_value)
    scores = product("iqhe,ikhe->ihqk", queries, key_rows) * head_width ** (-0.5)
    peak_score = jnp.max(scores, axis=-1, keepdims=True)
    total_log = peak_score + jnp.log(jnp.sum(jnp.exp(scores - peak_score), axis=-1, keepdims=True))
    attention = jnp.exp(scores - total_log)
    mixed_rows = product("ihqk,ikhe->iqhe", attention.astype(jnp.bfloat16), values).astype(
        jnp.bfloat16
    )
    mixed_rows = mixed_rows.reshape(item_count, row_count, local_heads * head_width)
    partials = product("ile,ed->ild", mixed_rows, weight_out)
    return (scatter_rows(partials), (hidden, queries, key_rows, values, total_log, mixed_rows))


def self_back(stream, norm_gain, weights, saved, upstream):
    weight_query, weight_key, weight_value, weight_out = weights
    hidden, queries, key_rows, values, total_log, mixed_rows = saved
    item_count, row_count, local_heads, head_width = queries.shape
    score_scale = head_width ** (-0.5)
    grad_all = gather_grads(upstream.astype(jnp.bfloat16))
    grad_mixed = product("ild,ed->ile", grad_all, weight_out).astype(jnp.bfloat16)
    grad_wout = product("ile,ild->ed", mixed_rows, grad_all)
    grad_heads = grad_mixed.reshape(item_count, row_count, local_heads, head_width)
    attention = jnp.exp(product("iqhe,ikhe->ihqk", queries, key_rows) * score_scale - total_log)
    grad_attention = product("iqhe,ikhe->ihqk", grad_heads, values)
    grad_values = product("ihqk,iqhe->ikhe", attention.astype(jnp.bfloat16), grad_heads).astype(
        jnp.bfloat16
    )
    row_delta = jnp.sum(attention * grad_attention, axis=-1, keepdims=True)
    grad_scores = (attention * (grad_attention - row_delta)).astype(jnp.bfloat16)
    grad_queries = (product("ihqk,ikhe->iqhe", grad_scores, key_rows) * score_scale).astype(
        jnp.bfloat16
    )
    grad_keys = (product("ihqk,iqhe->ikhe", grad_scores, queries) * score_scale).astype(
        jnp.bfloat16
    )

    def flatten(heads_array):
        return heads_array.reshape(item_count, row_count, local_heads * head_width)

    grad_wq = product("ild,ile->de", hidden, flatten(grad_queries))
    grad_wk = product("ild,ile->de", hidden, flatten(grad_keys))
    grad_wv = product("ild,ile->de", hidden, flatten(grad_values))
    grad_hidden = product("ile,de->ild", flatten(grad_queries), weight_query)
    grad_hidden = grad_hidden + product("ile,de->ild", flatten(grad_keys), weight_key)
    grad_hidden = grad_hidden + product("ile,de->ild", flatten(grad_values), weight_value)
    grad_stream, grad_gain = norm_back(stream, norm_gain, scatter_grads(grad_hidden))
    return (upstream + grad_stream, grad_gain, (grad_wq, grad_wk, grad_wv, grad_wout))


def body(
    latents,
    pixels,
    masks,
    cotangent,
    norm_latent,
    norm_pixel,
    norm_feed,
    norm_self,
    norm_last,
    cross_query,
    cross_key,
    cross_value,
    cross_out,
    feed_in,
    feed_out,
    self_query,
    self_key,
    self_value,
    self_out,
    last_in,
    last_out,
):
    full_query, full_key, full_value, full_out = (
        lax.all_gather(cross_query, "mp", axis=1, tiled=True),
        lax.all_gather(cross_key, "mp", axis=1, tiled=True),
        lax.all_gather(cross_value, "mp", axis=1, tiled=True),
        lax.all_gather(cross_out, "mp", axis=1, tiled=True),
    )
    latent_rows = latents.astype(jnp.float32)
    pixel_rows = pixels.astype(jnp.float32)
    inputs = layer_norm(pixel_rows, norm_pixel).astype(jnp.bfloat16)
    normed = layer_norm(latent_rows, norm_latent).astype(jnp.bfloat16)
    queries = gather_rows(product("iqd,de->iqe", normed, full_query).astype(jnp.bfloat16))
    key_rows = product("ikc,cd->ikd", inputs, full_key).astype(jnp.bfloat16)
    values = product("ikc,cd->ikd", inputs, full_value).astype(jnp.bfloat16)
    kept_slots = (masks > 0)[:, None, :]
    score_scale = D ** (-0.5)

    def cross_scores():
        return jnp.where(
            kept_slots, product("iqd,ikd->iqk", queries, key_rows) * score_scale, masked_score
        )

    scores = cross_scores()
    peak_score = jnp.max(scores, axis=-1, keepdims=True)
    row_total = jnp.sum(
        jnp.where(kept_slots, jnp.exp(scores - peak_score), 0.0), axis=-1, keepdims=True
    )
    peak_score, row_total = merged((peak_score, row_total), "mp", combine_stats)
    total_log = peak_score + jnp.log(row_total)
    attention = jnp.where(kept_slots, jnp.exp(scores - total_log), 0.0)
    partials = product("iqk,ikd->iqd", attention.astype(jnp.bfloat16), values)
    mixed_rows = lax.psum_scatter(
        partials.astype(jnp.bfloat16), "mp", scatter_dimension=1, tiled=True
    )
    state_one = latent_rows + product("iqd,de->iqe", mixed_rows, full_out)
    branch, feed_saved = feed_forward(state_one, norm_feed, feed_in, feed_out)
    state_two = state_one + branch
    branch, self_saved = self_forward(
        state_two, norm_self, self_query, self_key, self_value, self_out
    )
    state_three = state_two + branch
    branch, last_saved = feed_forward(state_three, norm_last, last_in, last_out)
    result = (state_three + branch).astype(jnp.bfloat16)
    upstream = cotangent.astype(jnp.float32)
    upstream, gain_last, grad_last_in, grad_last_out = feed_back(
        state_three, norm_last, last_in, last_out, last_saved, upstream
    )
    upstream, gain_self, self_grads = self_back(
        state_two, norm_self, (self_query, self_key, self_value, self_out), self_saved, upstream
    )
    upstream, gain_feed, grad_feed_in, grad_feed_out = feed_back(
        state_one, norm_feed, feed_in, feed_out, feed_saved, upstream
    )
    grad_branch = upstream.astype(jnp.bfloat16)
    grad_mixed = product("iqe,de->iqd", grad_branch, full_out).astype(jnp.bfloat16)
    grad_wout = product("iqd,iqe->de", mixed_rows, grad_branch)
    grad_mixed_all = gather_grads(grad_mixed)
    attention = jnp.where(kept_slots, jnp.exp(cross_scores() - total_log), 0.0)
    grad_attention = product("iqd,ikd->iqk", grad_mixed_all, values)
    grad_values = product("iqk,iqd->ikd", attention.astype(jnp.bfloat16), grad_mixed_all).astype(
        jnp.bfloat16
    )
    row_delta = lax.psum(jnp.sum(attention * grad_attention, axis=-1, keepdims=True), "mp")
    grad_scores = (attention * (grad_attention - row_delta)).astype(jnp.bfloat16)
    query_partials = product("iqk,ikd->iqd", grad_scores, key_rows) * score_scale
    grad_queries = lax.psum_scatter(
        query_partials.astype(jnp.bfloat16), "mp", scatter_dimension=1, tiled=True
    )
    grad_keys = (product("iqk,iqd->ikd", grad_scores, queries) * score_scale).astype(jnp.bfloat16)
    grad_wq = product("iqd,iqe->de", normed, grad_queries)
    grad_wk = product("ikc,ikd->cd", inputs, grad_keys)
    grad_wv = product("ikc,ikd->cd", inputs, grad_values)
    grad_normed = product("iqe,de->iqd", grad_queries, full_query)
    grad_own, gain_latent = norm_back(latent_rows, norm_latent, grad_normed)
    grad_latents = upstream + grad_own
    grad_inputs = product("ikd,cd->ikc", grad_keys, full_key) + product(
        "ikd,cd->ikc", grad_values, full_value
    )
    grad_pixels, gain_pixel = norm_back(pixel_rows, norm_pixel, grad_inputs)
    column_width = cross_query.shape[1]
    summed = lax.psum(
        (
            grad_wq,
            grad_wk,
            grad_wv,
            grad_wout,
            gain_latent,
            gain_pixel,
            gain_feed,
            gain_self,
            gain_last,
        ),
        ("dp", "mp"),
    )
    column_start = lax.axis_index("mp") * column_width
    cross_cols = tuple(
        (
            lax.dynamic_slice_in_dim(summed[index], column_start, column_width, 1)
            for index in range(4)
        )
    )
    gain_grads = summed[4:]
    shards = (
        lax.psum(grad_feed_in.astype(jnp.bfloat16), "dp").astype(jnp.float32),
        lax.psum(grad_feed_out.astype(jnp.bfloat16), "dp").astype(jnp.float32),
        lax.psum(self_grads[0].astype(jnp.bfloat16), "dp").astype(jnp.float32),
        lax.psum(self_grads[1].astype(jnp.bfloat16), "dp").astype(jnp.float32),
        lax.psum(self_grads[2].astype(jnp.bfloat16), "dp").astype(jnp.float32),
        lax.psum(self_grads[3].astype(jnp.bfloat16), "dp").astype(jnp.float32),
        lax.psum(grad_last_in.astype(jnp.bfloat16), "dp").astype(jnp.float32),
        lax.psum(grad_last_out.astype(jnp.bfloat16), "dp").astype(jnp.float32),
    )
    return (
        result,
        grad_latents,
        grad_pixels,
        gain_grads[0],
        gain_grads[1],
        gain_grads[2],
        gain_grads[3],
        gain_grads[4],
        cross_cols[0],
        cross_cols[1],
        cross_cols[2],
        cross_cols[3],
        shards[0],
        shards[1],
        shards[2],
        shards[3],
        shards[4],
        shards[5],
        shards[6],
        shards[7],
    )


def solution(mesh):
    placed = (
        P("dp", "mp", None),
        P("dp", "mp", None),
        P("dp", "mp"),
        P("dp", "mp", None),
        P(),
        P(),
        P(),
        P(),
        P(),
        P(None, "mp"),
        P(None, "mp"),
        P(None, "mp"),
        P(None, "mp"),
        P(None, "mp"),
        P("mp", None),
        P(None, "mp"),
        P(None, "mp"),
        P(None, "mp"),
        P("mp", None),
        P(None, "mp"),
        P("mp", None),
    )
    return jax.shard_map(
        body,
        mesh=mesh,
        in_specs=placed,
        out_specs=(
            P("dp", "mp", None),
            P("dp", "mp", None),
            P("dp", "mp", None),
            P(),
            P(),
            P(),
            P(),
            P(),
            P(None, "mp"),
            P(None, "mp"),
            P(None, "mp"),
            P(None, "mp"),
            P(None, "mp"),
            P("mp", None),
            P(None, "mp"),
            P(None, "mp"),
            P(None, "mp"),
            P("mp", None),
            P(None, "mp"),
            P("mp", None),
        ),
        check_vma=False,
    )
```

profile of v0, /device:TPU:1, one launch (start us, length us, event | category | flops | bytes accessed | tf_op | source)
XLA Modules:
  0.0 1229.7 jit_solution(12504638928603172198)
XLA Ops:
  10.3 43.4 %all-gather.15.cloned.1.call-done = bf16[1024,1024]{1,0:T(8,128)(2,1)} async-done(((bf16[1024,128]{1,0:T(8,128)(2,1)}), bf16[1024,1024]{1,0:T(8,128)(2,1)}) %all-gather.15.cloned.1.call-update) | async-done | bytes 2097168 | tf_op jit(solution)/shard_map/all_gather | solution.py:176
  53.7 2.9 fusion.32
  57.7 23.1 %all_gather.44 = bf16[261,1024]{1,0:T(8,128)(2,1)S(1)} all-gather(bf16[261,128]{1,0:T(8,128)(2,1)S(1)} %copy-done.66), channel_id=1, replica_groups=mesh['dp'=16,'mp'=8] {'mp'}, dimensions={1}, use_global_device_ids=true | all-gather | bytes 601344 | tf_op jit(solution)/shard_map/all_gather | solution.py:177
  80.8 26.5 %all_gather.47 = bf16[261,1024]{1,0:T(8,128)(2,1)S(1)} all-gather(bf16[261,128]{1,0:T(8,128)(2,1)S(1)} %copy-done.67), channel_id=1, replica_groups=mesh['dp'=16,'mp'=8] {'mp'}, dimensions={1}, use_global_device_ids=true | all-gather | bytes 601344 | tf_op jit(solution)/shard_map/all_gather | solution.py:178
  112.9 3.5 fusion.138
  116.9 22.5 %all-gather.3 = f32[8,2,512]{2,1,0:T(2,128)S(1)} all-gather(f32[1,2,512]{2,1,0:T(2,128)S(1)} %bitcast.221), channel_id=3, replica_groups=mesh['dp'=16,'mp'=8] {'mp'}, dimensions={0}, use_global_device_ids=true | all-gather | bytes 36864 | tf_op jit(solution)/shard_map/all_gather | solution.py:15
  139.4 22.5 %all-gather.2 = f32[8,2,512]{2,1,0:T(2,128)S(1)} all-gather(f32[1,2,512]{2,1,0:T(2,128)S(1)} %bitcast.220), channel_id=2, replica_groups=mesh['dp'=16,'mp'=8] {'mp'}, dimensions={0}, use_global_device_ids=true | all-gather | bytes 36864 | tf_op jit(solution)/shard_map/all_gather | solution.py:15
  162.4 4.3 convolution_convert_fusion.1
  166.9 58.8 %reduce-scatter.9.cloned.1.call-done = bf16[2,64,1024]{2,1,0:T(8,128)(2,1)} async-done(((bf16[2,512,1024]{2,1,0:T(8,128)(2,1)}), bf16[2,64,1024]{2,1,0:T(8,128)(2,1)}) %reduce-scatter.9.cloned.1.call-update) | async-done | bytes 262160 | tf_op jit(solution)/shard_map/reduce_scatter | solution.py:205
  229.1 40.5 %all-gather.21.cloned.1.call-done = bf16[2,512,1024]{2,1,0:T(8,128)(2,1)} async-done(((bf16[2,64,1024]{2,1,0:T(8,128)(2,1)}), bf16[2,512,1024]{2,1,0:T(8,128)(2,1)}) %all-gather.21.cloned.1.call-update) | async-done | bytes 2097168 | tf_op jit(solution)/shard_map/all_gather | solution.py:41
  274.8 41.8 %reduce-scatter.11.cloned.1.call-done = bf16[2,64,1024]{2,1,0:T(8,128)(2,1)} async-done(((bf16[2,512,1024]{2,1,0:T(8,128)(2,1)}), bf16[2,64,1024]{2,1,0:T(8,128)(2,1)}) %reduce-scatter.11.cloned.1.call-update) | async-done | bytes 262160 | tf_op jit(solution)/shard_map/reduce_scatter | solution.py:45
  319.0 40.4 %all-gather.23.cloned.1.call-done = bf16[2,512,1024]{2,1,0:T(8,128)(2,1)} async-done(((bf16[2,64,1024]{2,1,0:T(8,128)(2,1)}), bf16[2,512,1024]{2,1,0:T(8,128)(2,1)}) %all-gather.23.cloned.1.call-update) | async-done | bytes 2097168 | tf_op jit(solution)/shard_map/all_gather | solution.py:41
  369.6 41.6 %reduce-scatter.13.cloned.1.call-done = bf16[2,64,1024]{2,1,0:T(8,128)(2,1)} async-done(((bf16[2,512,1024]{2,1,0:T(8,128)(2,1)}), bf16[2,64,1024]{2,1,0:T(8,128)(2,1)}) %reduce-scatter.13.cloned.1.call-update) | async-done | bytes 262160 | tf_op jit(solution)/shard_map/reduce_scatter | solution.py:45
  414.6 40.2 %all-gather.25.cloned.1.call-done = bf16[2,512,1024]{2,1,0:T(8,128)(2,1)} async-done(((bf16[2,64,1024]{2,1,0:T(8,128)(2,1)}), bf16[2,512,1024]{2,1,0:T(8,128)(2,1)}) %all-gather.25.cloned.1.call-update) | async-done | bytes 2097168 | tf_op jit(solution)/shard_map/all_gather | solution.py:41
  454.8 3.1 fusion.91
  457.9 39.2 %all-gather.27.cloned.1.call-done = bf16[2,512,1024]{2,1,0:T(8,128)(2,1)} async-done(((bf16[2,64,1024]{2,1,0:T(8,128)(2,1)}), bf16[2,512,1024]{2,1,0:T(8,128)(2,1)}) %all-gather.27.cloned.1.call-update) | async-done | bytes 2097168 | tf_op jit(solution)/shard_map/all_gather | solution.py:51
  502.5 41.6 %reduce-scatter.17.cloned.1.call-done = bf16[2,64,1024]{2,1,0:T(8,128)(2,1)} async-done(((bf16[2,512,1024]{2,1,0:T(8,128)(2,1)}), bf16[2,64,1024]{2,1,0:T(8,128)(2,1)}) %reduce-scatter.17.cloned.1.call-update) | async-done | bytes 262160 | tf_op jit(solution)/shard_map/reduce_scatter | solution.py:55
  549.1 40.7 %all-gather.29.cloned.1.call-done = bf16[2,512,1024]{2,1,0:T(8,128)(2,1)} async-done(((bf16[2,64,1024]{2,1,0:T(8,128)(2,1)}), bf16[2,512,1024]{2,1,0:T(8,128)(2,1)}) %all-gather.29.cloned.1.call-update) | async-done | bytes 2097168 | tf_op jit(solution)/shard_map/all_gather | solution.py:51
  601.5 3.2 convolution_convert_fusion.6
  604.7 37.7 %reduce-scatter.19.cloned.1.call-done = bf16[2,64,1024]{2,1,0:T(8,128)(2,1)} async-done(((bf16[2,512,1024]{2,1,0:T(8,128)(2,1)}), bf16[2,64,1024]{2,1,0:T(8,128)(2,1)}) %reduce-scatter.19.cloned.1.call-update) | async-done | bytes 262160 | tf_op jit(solution)/shard_map/reduce_scatter | solution.py:55
  644.9 40.8 %reduce-scatter.15.cloned.1.call-done = bf16[2,64,1024]{2,1,0:T(8,128)(2,1)} async-done(((bf16[2,512,1024]{2,1,0:T(8,128)(2,1)}), bf16[2,64,1024]{2,1,0:T(8,128)(2,1)}) %reduce-scatter.15.cloned.1.call-update) | async-done | bytes 262160 | tf_op jit(solution)/shard_map/reduce_scatter | solution.py:45
  688.5 40.8 %all-gather.31.cloned.1.call-done = bf16[2,512,1024]{2,1,0:T(8,128)(2,1)} async-done(((bf16[2,64,1024]{2,1,0:T(8,128)(2,1)}), bf16[2,512,1024]{2,1,0:T(8,128)(2,1)}) %all-gather.31.cloned.1.call-update) | async-done | bytes 2097168 | tf_op jit(solution)/shard_map/all_gather | solution.py:51
  734.1 41.6 %reduce-scatter.21.cloned.1.call-done = bf16[2,64,1024]{2,1,0:T(8,128)(2,1)} async-done(((bf16[2,512,1024]{2,1,0:T(8,128)(2,1)}), bf16[2,64,1024]{2,1,0:T(8,128)(2,1)}) %reduce-scatter.21.cloned.1.call-update) | async-done | bytes 262160 | tf_op jit(solution)/shard_map/reduce_scatter | solution.py:55
  781.3 40.7 %all-gather.33.cloned.1.call-done = bf16[2,512,1024]{2,1,0:T(8,128)(2,1)} async-done(((bf16[2,64,1024]{2,1,0:T(8,128)(2,1)}), bf16[2,512,1024]{2,1,0:T(8,128)(2,1)}) %all-gather.33.cloned.1.call-update) | async-done | bytes 2097168 | tf_op jit(solution)/shard_map/all_gather | solution.py:51
  822.0 5.6 multiply_reduce_fusion
  827.6 15.1 %psum.126 = f32[2,512]{1,0:T(2,128)S(1)} all-reduce(f32[2,512]{1,0:T(2,128)S(1)} %get-tuple-element.256), channel_id=1, replica_groups=mesh['dp'=16,'mp'=8] {'mp'}, use_global_device_ids=true, to_apply=%region_31.32 | all-reduce | flops 1024 | bytes 8192 | tf_op jit(solution)/shard_map/psum | solution.py:236
  850.2 3.2 fusion.28
  876.8 16.0 %reduce-scatter.23.cloned.1.call-done = bf16[2,64,1024]{2,1,0:T(8,128)(2,1)} async-done(((bf16[2,512,1024]{2,1,0:T(8,128)(2,1)}), bf16[2,64,1024]{2,1,0:T(8,128)(2,1)}) %reduce-scatter.23.cloned.1.call-update) | async-done | bytes 262160 | tf_op jit(solution)/shard_map/reduce_scatter | solution.py:239
  892.9 3.7 convolution_bitcast_fusion.1
  896.6 148.9 %all-reduce.8.cloned.1.call-done = (bf16[1024,128]{1,0:T(8,128)(2,1)}, bf16[128,1024]{1,0:T(8,128)(2,1)}, bf16[1024,128]{1,0:T(8,128)(2,1)}, bf16[1024,128]{1,0:...) async-done(((bf16[1024,128]{1,0:T(8,128)(2,1)}, bf16[128,1024]{1,0:T(8,128)(2,1)}, ...) | async-done | bytes 2097168 | tf_op jit(solution)/shard_map/psum | solution.py:277
  1061.2 68.2 %all-reduce = (f32[1024]{0:T(1024)}, f32[261]{0:T(512)}, f32[1024]{0:T(1024)}, f32[1024]{0:T(1024)}, f32[1024]{0:T(1024)}) all-reduce(f32[1024]{0:T(1024)S(1)} %get-tuple-element.208, f32[261]{0:T(512)S(1)} %get-tuple-element.200, f32[1024]{0:T(1024)S(1)} %get-tuple-element.206, ...), channel_id=1, replica_groups=mesh['dp'=16,'mp'=8] {'dp','mp'}, use_global_device_ids=true, to_apply=%region_38.39 | all-reduce | flops 4357 | bytes 34856 | tf_op jit(solution)/shard_map/psum | solution.py:254
  1130.5 88.0 %all-reduce.6.cloned.1.call-done = (f32[1024,1024]{1,0:T(8,128)}, f32[261,1024]{1,0:T(8,128)}, f32[261,1024]{1,0:T(8,128)}, f32[1024,1024]{1,0:T(8,128)}) async-done(((f32[1024,1024]{1,0:T(8,128)}, f32[261,1024]{1,0:T(8,128)}, f32[261,1024]{1,0:T(8,128)}, f32[1024,1024]{1,0:T(8,128)}), (f32[1024,1024]{1,0:T(8,128)}, f32[261,1024]{1,0:T(8,128)}, f32[261,1024]{1,0:T(8,128)}, ...) | async-done | bytes 10526736 | tf_op jit(solution)/shard_map/psum | solution.py:254
  (319 shorter events, 124.1 us)
Async XLA Ops:
  7.2 447.6 %copy-start = (bf16[1024,128]{1,0:T(8,128)(2,1)S(1)}, bf16[1024,128]{1,0:T(8,128)(2,1)}, u32[]{:S(2)}) copy-start(bf16[1024,128]{1,0:T(8,128)(2,1)} %param.42) | copy-start | bytes 786436
  7.2 50.2 %copy-start.71 = (s32[2,512]{1,0:T(2,128)S(1)}, s32[2,512]{1,0:T(2,128)}, u32[]{:S(2)}) copy-start(s32[2,512]{1,0:T(2,128)} %param.25) | copy-start | bytes 12292
  7.2 50.2 %copy-start.9 = (bf16[2,512,261]{1,0,2:T(2,128)(2,1)S(1)}, bf16[2,512,261]{1,0,2:T(2,128)(2,1)}, u32[]{:S(2)}) copy-start(bf16[2,512,261]{1,0,2:T(2,128)(2,1)} %param.24) | copy-start | bytes 1603588
  7.2 46.5 %all-gather.15.cloned.1.call-start = ((), (), s32[]{:S(2)}) async-start(), calls=%async_computation.8 | async-start | bytes 2359296 | tf_op jit(solution)/shard_map/all_gather | solution.py:176
  8.0 105.0 %all-gather.17.cloned.1.call-start = ((), (), s32[]{:S(2)}) async-start(), calls=%async_computation.9 | async-start | bytes 2359296 | tf_op jit(solution)/shard_map/all_gather | solution.py:41
  10.3 47.5 %copy-start.66 = (bf16[261,128]{1,0:T(8,128)(2,1)S(1)}, bf16[261,128]{1,0:T(8,128)(2,1)}, u32[]{:S(2)}) copy-start(bf16[261,128]{1,0:T(8,128)(2,1)} %param.33) | copy-start | bytes 200452
  10.3 70.5 %copy-start.67 = (bf16[261,128]{1,0:T(8,128)(2,1)S(1)}, bf16[261,128]{1,0:T(8,128)(2,1)}, u32[]{:S(2)}) copy-start(bf16[261,128]{1,0:T(8,128)(2,1)} %param.34) | copy-start | bytes 200452
  10.3 97.0 %copy-start.70 = (f32[261]{0:T(512)S(1)}, f32[261]{0:T(512)}, u32[]{:S(2)}) copy-start(f32[261]{0:T(512)} %param.28) | copy-start | bytes 3136
  56.7 110.2 %all-gather.19.cloned.1.call-start = ((), (), s32[]{:S(2)}) async-start(), calls=%async_computation.11 | async-start | bytes 2359296 | tf_op jit(solution)/shard_map/all_gather | solution.py:179
  57.4 168.3 %reduce-scatter.9.cloned.1.call-start = ((), (), s32[]{:S(2)}) async-start(), calls=%async_computation.10 | async-start | bytes 2359296 | tf_op jit(solution)/shard_map/reduce_scatter | solution.py:205
  116.5 45.9 %copy-start.13 = (f32[2,512,512]{1,2,0:T(8,128)}, f32[2,512,512]{1,2,0:T(8,128)S(1)}, u32[]{:S(2)}) copy-start(f32[2,512,512]{1,2,0:T(8,128)S(1)} %get-tuple-element.249) | copy-start | bytes 6291460
  166.8 58.9 %copy-start.6 = (bf16[2,64,1024]{2,1,0:T(8,128)(2,1)S(1)}, bf16[2,64,1024]{2,1,0:T(8,128)(2,1)}, u32[]{:S(2)}) copy-start(bf16[2,64,1024]{2,1,0:T(8,128)(2,1)} %param.23) | copy-start | bytes 786436
  166.8 61.4 %copy-start.69 = (f32[1024]{0:T(1024)S(1)}, f32[1024]{0:T(1024)}, u32[]{:S(2)}) copy-start(f32[1024]{0:T(1024)} %param.29) | copy-start | bytes 12292
  166.8 102.8 %copy-start.52 = (bf16[1024,128]{1,0:T(8,128)(2,1)S(1)}, bf16[1024,128]{1,0:T(8,128)(2,1)}, u32[]{:S(2)}) copy-start(bf16[1024,128]{1,0:T(8,128)(2,1)} %param.36) | copy-start | bytes 786436
  166.8 102.8 %all-gather.21.cloned.1.call-start = ((), (), s32[]{:S(2)}) async-start(), calls=%async_computation.12 | async-start | bytes 2359296 | tf_op jit(solution)/shard_map/all_gather | solution.py:41
  229.0 87.6 %reduce-scatter.11.cloned.1.call-start = ((), (), s32[]{:S(2)}) async-start(), calls=%async_computation.13 | async-start | bytes 2359296 | tf_op jit(solution)/shard_map/reduce_scatter | solution.py:45
  274.7 84.7 %all-gather.23.cloned.1.call-start = ((), (), s32[]{:S(2)}) async-start(), calls=%async_computation.14 | async-start | bytes 2359296 | tf_op jit(solution)/shard_map/all_gather | solution.py:41
  318.8 92.4 %reduce-scatter.13.cloned.1.call-start = ((), (), s32[]{:S(2)}) async-start(), calls=%async_computation.15 | async-start | bytes 2359296 | tf_op jit(solution)/shard_map/reduce_scatter | solution.py:45
  369.5 85.3 %all-gather.25.cloned.1.call-start = ((), (), s32[]{:S(2)}) async-start(), calls=%async_computation.16 | async-start | bytes 2359296 | tf_op jit(solution)/shard_map/all_gather | solution.py:41
  414.0 83.2 %all-gather.27.cloned.1.call-start = ((), (), s32[]{:S(2)}) async-start(), calls=%async_computation.18 | async-start | bytes 2359296 | tf_op jit(solution)/shard_map/all_gather | solution.py:51
  414.5 129.6 %reduce-scatter.17.cloned.1.call-start = ((), (), s32[]{:S(2)}) async-start(), calls=%async_computation.19 | async-start | bytes 2359296 | tf_op jit(solution)/shard_map/reduce_scatter | solution.py:55
  502.5 87.3 %all-gather.29.cloned.1.call-start = ((), (), s32[]{:S(2)}) async-start(), calls=%async_computation.20 | async-start | bytes 2359296 | tf_op jit(solution)/shard_map/all_gather | solution.py:51
  549.0 93.4 %reduce-scatter.19.cloned.1.call-start = ((), (), s32[]{:S(2)}) async-start(), calls=%async_computation.21 | async-start | bytes 2359296 | tf_op jit(solution)/shard_map/reduce_scatter | solution.py:55
  600.6 85.1 %reduce-scatter.15.cloned.1.call-start = ((), (), s32[]{:S(2)}) async-start(), calls=%async_computation.17 | async-start | bytes 2359296 | tf_op jit(solution)/shard_map/reduce_scatter | solution.py:45
  604.6 81.1 %copy-start.19 = (bf16[2,64,1024]{2,1,0:T(8,128)(2,1)S(1)}, bf16[2,64,1024]{2,1,0:T(8,128)(2,1)}, u32[]{:S(2)}) copy-start(bf16[2,64,1024]{2,1,0:T(8,128)(2,1)} %reduce-scatter.17.cloned.1.call-done) | copy-start | bytes 786436
  604.7 124.6 %all-gather.31.cloned.1.call-start = ((), (), s32[]{:S(2)}) async-start(), calls=%async_computation.22 | async-start | bytes 2359296 | tf_op jit(solution)/shard_map/all_gather | solution.py:51
  688.4 87.3 %reduce-scatter.21.cloned.1.call-start = ((), (), s32[]{:S(2)}) async-start(), calls=%async_computation.23 | async-start | bytes 2359296 | tf_op jit(solution)/shard_map/reduce_scatter | solution.py:55
  734.0 88.0 %all-gather.33.cloned.1.call-start = ((), (), s32[]{:S(2)}) async-start(), calls=%async_computation.24 | async-start | bytes 2359296 | tf_op jit(solution)/shard_map/all_gather | solution.py:51
  781.2 111.7 %reduce-scatter.23.cloned.1.call-start = ((), (), s32[]{:S(2)}) async-start(), calls=%async_computation.25 | async-start | bytes 2359296 | tf_op jit(solution)/shard_map/reduce_scatter | solution.py:239
  849.3 196.3 %all-reduce.8.cloned.1.call-start = ((), (), s32[]{:S(2)}) async-start(), calls=%async_computation.27 | async-start | bytes 4194304 | tf_op jit(solution)/shard_map/psum | solution.py:277
  863.9 354.6 %all-reduce.6.cloned.1.call-start = ((), (), s32[]{:S(2)}) async-start(), calls=%async_computation.26 | async-start | bytes 21102592 | tf_op jit(solution)/shard_map/psum | solution.py:254
  1129.4 93.0 %copy-start.1 = (bf16[1024,128]{1,0:T(8,128)(2,1)S(1)}, bf16[1024,128]{1,0:T(8,128)(2,1)}, u32[]{:S(2)}) copy-start(bf16[1024,128]{1,0:T(8,128)(2,1)} %param.42) | copy-start | bytes 786436
  (65 other events, 416.3 us)
Sparse Core Ops, SparseCore 0:
  9.6 44.0 all-gather.14
  56.8 50.2 all-gather.16
  108.7 40.9 all-gather.18
  166.9 58.7 reduce-scatter.8
  229.2 40.3 all-gather.20
  274.8 41.7 reduce-scatter.10
  318.9 40.4 all-gather.22
  369.7 41.5 reduce-scatter.12
  414.1 40.7 all-gather.24
  456.3 40.7 all-gather.26
  502.6 41.5 reduce-scatter.16
  549.1 40.6 all-gather.28
  600.7 41.6 reduce-scatter.18
  644.7 40.9 reduce-scatter.14
  688.5 40.7 all-gather.30
  734.1 41.5 reduce-scatter.20
  781.3 40.5 all-gather.32
  849.4 43.4 reduce-scatter.22
  897.1 148.4 all-reduce.7
  1051.1 167.3 all-reduce.5
where the time goes:
time: 1240 us; the launch traced here: 1230 us
  waiting for transfers between devices  885 us (71%)
  blocking collectives  178 us (14%)
  matrix products  93.5 us (8%)
  other arithmetic  38.2 us (3%)
  local copies, waits for them, and re-layouts  17.9 us (1%)
  between operations  15.5 us (1%)
    all_gather x4, waiting for transfers between devices, gather_grads(): return lax.all_gather(pieces, 'mp', axis=1, tiled=True)  161 us
    psum x1, waiting for transfers between devices, body(): lax.psum(grad_feed_in.astype(jnp.bfloat16), 'dp').astype(jnp.float32)  149 us
    reduce_scatter x3, waiting for transfers between devices, scatter_rows(): lax.psum_scatter(partials.astype(jnp.bfloat16), 'mp', scatter_dimension=1...  124 us
    all_gather x4, waiting for transfers between devices, gather_rows(): return lax.all_gather(pieces, 'mp', axis=1, tiled=True)  121 us
    reduce_scatter x3, waiting for transfers between devices, scatter_grads(): lax.psum_scatter(partials.astype(jnp.bfloat16), 'mp', scatter_dimension=1...  121 us
    dot_general x48, matrix products, product(): jnp.einsum(pattern, left_side, right_side, preferred_element_type=jnp.flo...  93.5 us
    psum x1, waiting for transfers between devices, body(): lax.psum((grad_wq, grad_wk, grad_wv, grad_wout, gain_latent, gain_pixel,...  88 us
    psum x1, blocking collectives, body(): lax.psum((grad_wq, grad_wk, grad_wv, grad_wout, gain_latent, gain_pixel,...  68.2 us
  transfers between devices with their start and end apart: 20, of which 18 were waited for; matrix products, arithmetic and copies ran while one was open for 5% of the time, Pallas kernels for 0%

commit v1 on v0

v1 whole, which is shorter than its diff:
```python
import jax
import jax.numpy as jnp
from jax import lax
from jax.sharding import PartitionSpec as P

D = 1024
C = 261
CP = 272
CH = 288
HALF = 144
HEADS = 8
HEAD = 128
MP = 8
ITEMS = 2
ROWS = 64
LOCAL = ITEMS * ROWS
SLOTS = 512
NLAT = 512
WIDE = 512
MEMBERS = 64
PART = 40
EPS = 1e-05
MASKED = -1e30
GELU_A = 0.044715
GELU_K = 0.7978845608028654

bf16 = jnp.bfloat16
f32 = jnp.float32

SWAP = [(i, i ^ 1) for i in range(16)]
CHIPS = [
    [(d * 2 + core) * MP + m for d in range(8) for m in range(MP)] for core in range(2)
]
COPIES = [[d * 2 + core for d in range(8)] for core in range(2)]


def dot(a, b):
    return lax.dot_general(a, b, (((1,), (0,)), ((), ())), preferred_element_type=f32)


def dot_t(a, b):
    return lax.dot_general(a, b, (((1,), (1,)), ((), ())), preferred_element_type=f32)


def t_dot(a, b):
    return dot(a.T, b)


def core_swap(x):
    return lax.ppermute(x, "dp", SWAP)


def exchange(x):
    return lax.all_to_all(x, "mp", 0, 0, tiled=True)


def to_all(x):
    return exchange(jnp.broadcast_to(x[None], (MP,) + x.shape))


def normal(v):
    center = v - jnp.mean(v, axis=-1, keepdims=True)
    spread = jnp.mean(center * center, axis=-1, keepdims=True)
    scale = lax.rsqrt(spread + EPS)
    return center * scale, scale


def normal_back(unit, scale, gain, upstream):
    grad_gain = jnp.sum(upstream * unit, axis=0, keepdims=True)
    grad_unit = upstream * gain
    inner = jnp.mean(grad_unit * unit, axis=-1, keepdims=True)
    grad = scale * (grad_unit - jnp.mean(grad_unit, axis=-1, keepdims=True) - unit * inner)
    return grad, grad_gain


def gelu_parts(v):
    square = v * v
    t = jnp.tanh(GELU_K * v * (1.0 + GELU_A * square))
    value = 0.5 * v * (1.0 + t)
    slope = 0.5 * (1.0 + t) + 0.5 * v * (1.0 - t * t) * GELU_K * (1.0 + 3.0 * GELU_A * square)
    return value, slope


def split3(v):
    high = v.astype(bf16)
    rest = v - high.astype(f32)
    middle = rest.astype(bf16)
    low = (rest - middle.astype(f32)).astype(bf16)
    return [high.astype(f32), middle.astype(f32), low.astype(f32)]


def join3(rows, start):
    return rows[start : start + 1] + rows[start + 1 : start + 2] + rows[start + 2 : start + 3]


def halves(core, own, other, axis):
    first = jnp.where(core == 0, own, other)
    second = jnp.where(core == 0, other, own)
    return jnp.concatenate([first, second], axis=axis)


def pick(core, v, own):
    take_low = core == 0 if own else core != 0
    return jnp.where(take_low, v[:, :WIDE], v[:, WIDE:])


def times_in(core, x, own, other):
    return dot_t(pick(core, x, True), own) + dot_t(pick(core, x, False), other)


def times_out(core, x, own, other):
    return halves(core, dot(x, own), dot(x, other), 1)


def feed_forward(core, stream, gain, win, wout):
    unit, scale = normal(stream)
    hidden = (unit * gain).astype(bf16)
    before = times_in(core, hidden, *win)
    active, slope = gelu_parts(before)
    active = active.astype(bf16)
    return times_out(core, active, *wout), (hidden, active, slope)


def feed_back(core, stream, gain, win, wout, saved, upstream):
    hidden, active, slope = saved
    dy = upstream.astype(bf16)
    grad_active = times_in(core, dy, *wout)
    grad_before = (grad_active * slope).astype(bf16)
    grad_hidden = times_out(core, grad_before, *win)
    unit, scale = normal(stream)
    grad, grad_gain = normal_back(unit, scale, gain, grad_hidden)
    return upstream + grad, grad_gain, dy, grad_before


def weight_grad(core, left, right):
    flipped = left.T
    own = dot(flipped, pick(core, right, True)).astype(bf16)
    other = dot(flipped, pick(core, right, False)).astype(bf16)
    return own.reshape(MP, HEAD, WIDE), other.reshape(MP, HEAD, WIDE)


def by_item(x):
    parts = x.reshape(MP, CP, ITEMS, ROWS)
    return [parts[:, :, i].transpose(1, 0, 2).reshape(CP, NLAT) for i in range(ITEMS)]


def by_peer(items):
    parts = jnp.stack([v.reshape(CP, MP, ROWS) for v in items], axis=2)
    return parts.transpose(1, 0, 2, 3).reshape(MP, CP, LOCAL)


def rows_of(x, item):
    return x.reshape(MP, ITEMS, ROWS, HEAD)[:, item].reshape(NLAT, HEAD)


def rows_back(items):
    return jnp.stack([v.reshape(MP, ROWS, HEAD) for v in items], axis=1).reshape(
        MP * LOCAL, HEAD
    )


def body(
    latents,
    pixels,
    masks,
    cotangent,
    norm_latent,
    norm_pixel,
    norm_feed,
    norm_self,
    norm_last,
    cross_query,
    cross_key,
    cross_value,
    cross_out,
    feed_in,
    feed_out,
    self_query,
    self_key,
    self_value,
    self_out,
    last_in,
    last_out,
):
    core = lax.axis_index("dp") % 2
    mine = lax.axis_index("mp")
    row_ids = lax.broadcasted_iota(jnp.int32, (CP, 1), 0)
    gain_latent, gain_feed, gain_self, gain_last = (
        g[None, :] for g in (norm_latent, norm_feed, norm_self, norm_last)
    )

    def own_half(x, keep):
        low, high = x[:, :WIDE], x[:, WIDE:]
        return jnp.where((core == 0) == keep, low, high)

    def gather_pack(weights):
        pack = jnp.stack([own_half(w, True) for w in weights])
        own = lax.all_gather(pack, "mp")
        other = core_swap(own)
        return [
            (own[:, j].reshape(D, WIDE), other[:, j].reshape(D, WIDE))
            for j in range(len(weights))
        ]

    win, wout = gather_pack([feed_in.T, feed_out])
    wself, last_win, last_wout = gather_pack([self_out, last_in.T, last_out])

    key_rows = jnp.pad(cross_key, ((0, CH - C), (0, 0)))
    value_rows = jnp.pad(cross_value, ((0, CH - C), (0, 0)))

    def core_rows(x):
        return jnp.where(core == 0, x[:HALF], x[HALF:])

    partial = dot_t(core_rows(key_rows), cross_query).astype(bf16)
    partial = partial.reshape(HALF, MP, HEAD).transpose(1, 0, 2)
    shared = jnp.broadcast_to(core_rows(value_rows)[None], (MP, HALF, HEAD))
    got = exchange(jnp.concatenate([partial, shared], axis=1))
    score_part = jnp.sum(got[:, :HALF].astype(f32), axis=0).astype(bf16)
    value_half = got[:, HALF:].transpose(1, 0, 2).reshape(HALF, D)
    mix_part = dot(value_half, cross_out).astype(bf16)
    got = to_all(jnp.concatenate([score_part, mix_part], axis=0))
    merged = got.reshape(MP, 2, HALF, HEAD).transpose(1, 2, 0, 3).reshape(2, HALF, D)
    merged = jnp.concatenate([merged, value_half[None]], axis=0)
    crossed = core_swap(merged)
    score_map, mix_map, value_full = (
        halves(core, merged[j], crossed[j], 0)[:CP] for j in range(3)
    )

    latent_rows = latents.reshape(LOCAL, D).astype(f32)
    latent_unit, latent_scale = normal(latent_rows)
    normed = (latent_unit * gain_latent).astype(bf16)
    asked = dot_t(score_map, normed) * (D**-0.5)
    asked = jnp.where(row_ids < C, asked, jnp.where(row_ids == C, 1.0, 0.0)).astype(bf16)
    asked_all = by_item(to_all(asked))

    pixel_rows = pixels.reshape(ITEMS * SLOTS, C).astype(f32)
    pixel_unit, pixel_scale = normal(pixel_rows)
    gain_pixel = norm_pixel[None, :]
    inputs = (pixel_unit * gain_pixel).astype(bf16)
    bias = jnp.where(masks.reshape(ITEMS * SLOTS, 1) > 0, 0.0, MASKED).astype(bf16)
    inputs = jnp.concatenate(
        [inputs, bias, jnp.zeros((ITEMS * SLOTS, CP - C - 1), bf16)], axis=1
    ).reshape(ITEMS, SLOTS, CP)

    sums = []
    for i in range(ITEMS):
        scores = dot(inputs[i], asked_all[i])
        peak = jnp.max(scores, axis=0, keepdims=True)
        weight = jnp.exp(scores - peak)
        total = jnp.sum(weight, axis=0, keepdims=True)
        mixed = t_dot(inputs[i], weight.astype(bf16))
        mixed = jnp.where(row_ids < C, mixed, 0.0)
        for offset, row in enumerate(split3(peak) + split3(total)):
            mixed = jnp.where(row_ids == C + 1 + offset, row, mixed)
        sums.append(mixed.astype(bf16))
    got = exchange(by_peer(sums)).astype(f32)
    peaks = [join3(got[s], C + 1) for s in range(MP)]
    totals = [join3(got[s], C + 4) for s in range(MP)]
    peak = peaks[0]
    for s in range(1, MP):
        peak = jnp.maximum(peak, peaks[s])
    total, mixed = 0.0, 0.0
    for s in range(MP):
        share = jnp.exp(peaks[s] - peak)
        total = total + share * totals[s]
        mixed = mixed + share * got[s]
    mixed = jnp.where(row_ids < C, mixed / total, 0.0)
    lse = peak + jnp.log(total)
    mixed_low = mixed.astype(bf16)

    state_one = latent_rows + t_dot(mixed_low, mix_map)
    branch, feed_saved = feed_forward(core, state_one, gain_feed, win, wout)
    state_two = state_one + branch
    self_unit, self_scale = normal(state_two)
    hidden = (self_unit * gain_self).astype(bf16)

    hidden_all = to_all(hidden).reshape(MP * LOCAL, D)
    queries, keys, values = (
        dot(hidden_all, w).astype(bf16) for w in (self_query, self_key, self_value)
    )
    head_scale = HEAD**-0.5
    outs, logs = [], []
    for i in range(ITEMS):
        q, k, v = rows_of(queries, i), rows_of(keys, i), rows_of(values, i)
        scores = dot_t(k, q) * head_scale
        top = jnp.max(scores, axis=0, keepdims=True)
        log = top + jnp.log(jnp.sum(jnp.exp(scores - top), axis=0, keepdims=True))
        attention = jnp.exp(scores - log).astype(bf16)
        outs.append(dot(v.T, attention).T.astype(bf16))
        logs.append(log)
    got = exchange(rows_back(outs).reshape(MP, LOCAL, HEAD))
    heads_out = got.transpose(1, 0, 2).reshape(LOCAL, D)
    state_three = state_two + times_out(core, heads_out, *wself)
    branch, last_saved = feed_forward(core, state_three, gain_last, last_win, last_wout)
    result = (state_three + branch).astype(bf16)

    upstream = cotangent.reshape(LOCAL, D).astype(f32)
    upstream, grad_gain_last, dy, grad_before = feed_back(
        core, state_three, gain_last, last_win, last_wout, last_saved, upstream
    )
    grad_last_out = weight_grad(core, last_saved[1], dy)
    grad_last_in = weight_grad(core, grad_before, last_saved[0])
    dy = upstream.astype(bf16)
    grad_heads = times_in(core, dy, *wself).astype(bf16)
    grad_self_out = weight_grad(core, heads_out, dy)

    got = exchange(grad_heads.reshape(LOCAL, MP, HEAD).transpose(1, 0, 2))
    grad_heads = got.reshape(MP * LOCAL, HEAD)
    dqs, dks, dvs = [], [], []
    for i in range(ITEMS):
        q, k, v = rows_of(queries, i), rows_of(keys, i), rows_of(values, i)
        g = rows_of(grad_heads, i)
        attention = jnp.exp(dot_t(k, q) * head_scale - logs[i])
        grad_attention = dot_t(v, g)
        delta = jnp.sum(attention * grad_attention, axis=0, keepdims=True)
        dvs.append(dot(attention.astype(bf16), g).astype(bf16))
        grad_scores = (attention * (grad_attention - delta)).astype(bf16)
        dks.append((dot(grad_scores, q) * head_scale).astype(bf16))
        dqs.append((dot(k.T, grad_scores).T * head_scale).astype(bf16))
    grad_query, grad_key, grad_value = rows_back(dqs), rows_back(dks), rows_back(dvs)
    grad_hidden = (
        dot_t(grad_query, self_query)
        + dot_t(grad_key, self_key)
        + dot_t(grad_value, self_value)
    )
    flipped = hidden_all.T
    grad_qkv = [dot(flipped, g) for g in (grad_query, grad_key, grad_value)]
    got = exchange(grad_hidden.astype(bf16).reshape(MP, LOCAL, D))
    grad_hidden = jnp.sum(got.astype(f32), axis=0)
    grad, grad_gain_self = normal_back(self_unit, self_scale, gain_self, grad_hidden)
    upstream = upstream + grad
    upstream, grad_gain_feed, dy, grad_before = feed_back(
        core, state_one, gain_feed, win, wout, feed_saved, upstream
    )
    grad_feed_out = weight_grad(core, feed_saved[1], dy)
    grad_feed_in = weight_grad(core, grad_before, feed_saved[0])
    dy = upstream.astype(bf16)
    grad_mixed = dot_t(mix_map, dy)
    delta = jnp.sum(grad_mixed * mixed, axis=0, keepdims=True)
    mix_sum = dot(mixed_low, dy)
    sent = jnp.where(row_ids < C, grad_mixed, 0.0)
    for offset, row in enumerate(split3(lse) + split3(delta)):
        sent = jnp.where(row_ids == C + 1 + offset, row, sent)
    told_all = by_item(to_all(sent.astype(bf16)))

    partials, grad_inputs = [], []
    for i in range(ITEMS):
        told = told_all[i].astype(f32)
        log, delta = join3(told, C + 1), join3(told, C + 4)
        grad_mixed_all = jnp.where(row_ids < C, told, 0.0).astype(bf16)
        attention = jnp.exp(dot(inputs[i], asked_all[i]) - log)
        grad_attention = dot(inputs[i], grad_mixed_all)
        grad_scores = (attention * (grad_attention - delta)).astype(bf16)
        grad_inputs.append(
            dot_t(grad_scores, asked_all[i]) + dot_t(attention.astype(bf16), grad_mixed_all)
        )
        partials.append(t_dot(inputs[i], grad_scores).astype(bf16))
    got = exchange(by_peer(partials))
    grad_asked = jnp.sum(got.astype(f32), axis=0) * (D**-0.5)
    grad_asked = jnp.where(row_ids < C, grad_asked, 0.0).astype(bf16)
    score_sum = dot(grad_asked, normed)
    grad_normed = t_dot(grad_asked, score_map)
    grad, grad_gain_latent = normal_back(latent_unit, latent_scale, gain_latent, grad_normed)
    grad_latents = upstream + grad
    grad_inputs = jnp.concatenate(grad_inputs, axis=0)[:, :C]
    grad_pixels, grad_gain_pixel = normal_back(
        pixel_unit, pixel_scale, gain_pixel, grad_inputs
    )

    gains = jnp.concatenate(
        [
            grad_gain_latent,
            grad_gain_feed,
            grad_gain_self,
            grad_gain_last,
            jnp.pad(grad_gain_pixel, ((0, 0), (0, D - C))),
        ],
        axis=0,
    )
    high = gains.astype(bf16)
    low = (gains - high.astype(f32)).astype(bf16)
    both = jnp.concatenate([high, low], axis=0)
    score_sum = jnp.concatenate([score_sum[:C].astype(bf16), both], axis=0)
    score_sum = jnp.pad(score_sum, ((0, MP * PART - C - 10), (0, 0)))
    mix_sum = jnp.pad(mix_sum.astype(bf16), ((0, MP * PART - CP), (0, 0)))
    kept = jnp.where(core == 0, score_sum, mix_sum)
    given = jnp.where(core == 0, mix_sum, score_sum)
    total = kept.astype(f32) + core_swap(given).astype(f32)
    total = total.astype(bf16).reshape(MP, PART, MP, HEAD).transpose(0, 2, 1, 3)
    got = lax.all_to_all(
        total.reshape(MEMBERS, PART, HEAD),
        ("dp", "mp"),
        0,
        0,
        tiled=True,
        axis_index_groups=CHIPS,
    )
    total = jnp.sum(got.astype(f32), axis=0).astype(bf16)
    got = lax.all_to_all(
        jnp.broadcast_to(total[None], (MEMBERS, PART, HEAD)),
        ("dp", "mp"),
        0,
        0,
        tiled=True,
        axis_index_groups=CHIPS,
    )
    total = got.reshape(MP, MP, PART, HEAD).transpose(0, 2, 1, 3).reshape(MP * PART, D)
    crossed = core_swap(total)
    score_sum = jnp.where(core == 0, total, crossed)
    mix_sum = jnp.where(core == 0, crossed, total)[:CP]
    both = score_sum[C : C + 10].astype(f32)
    gains = both[:5] + both[5:]
    score_sum = score_sum[:CP]
    out_rows = lax.all_to_all(
        cross_out.reshape(MP, HEAD, HEAD), "mp", 0, 0, tiled=True
    )
    out_rows = out_rows.transpose(1, 0, 2).reshape(HEAD, D)
    grad_cross_query = t_dot(score_sum, key_rows[:CP])
    grad_cross_key = dot(score_sum, cross_query)[:C]
    own_mix = lax.dynamic_slice_in_dim(mix_sum, mine * HEAD, HEAD, 1)
    grad_cross_out = t_dot(value_full, own_mix)
    grad_cross_value = dot_t(mix_sum, out_rows)[:C]

    def reduce_pack(pairs):
        own = jnp.stack([p[0] for p in pairs], axis=1)
        other = jnp.stack([p[1] for p in pairs], axis=1)
        pack = (own.astype(f32) + core_swap(other).astype(f32)).astype(bf16)
        pack = lax.psum_scatter(pack, "mp")
        pack = lax.psum(pack, "dp", axis_index_groups=COPIES)
        crossed = core_swap(pack)
        return [
            halves(core, pack[j], crossed[j], 1).astype(f32) for j in range(len(pairs))
        ]

    grad_self_out, grad_last_in, grad_last_out = reduce_pack(
        [grad_self_out, grad_last_in, grad_last_out]
    )
    grad_feed_in, grad_feed_out = reduce_pack([grad_feed_in, grad_feed_out])
    grad_qkv = lax.psum(jnp.stack(grad_qkv).astype(bf16), "dp").astype(f32)
    shape = (ITEMS, ROWS, D)
    return (
        result.reshape(shape),
        grad_latents.reshape(shape),
        grad_pixels.reshape(ITEMS, SLOTS, C),
        gains[0],
        gains[4, :C],
        gains[1],
        gains[2],
        gains[3],
        grad_cross_query,
        grad_cross_key,
        grad_cross_value,
        grad_cross_out,
        grad_feed_in.T,
        grad_feed_out,
        grad_qkv[0],
        grad_qkv[1],
        grad_qkv[2],
        grad_self_out,
        grad_last_in.T,
        grad_last_out,
    )


def solution(mesh):
    rows = P("dp", "mp", None)
    columns = P(None, "mp")
    depth = P("mp", None)
    return jax.shard_map(
        body,
        mesh=mesh,
        in_specs=(rows, rows, P("dp", "mp"), rows)
        + (P(),) * 5
        + (columns,) * 5
        + (depth,)
        + (columns,) * 3
        + (depth, columns, depth),
        out_specs=(rows,) * 3
        + (P(),) * 5
        + (columns,) * 5
        + (depth,)
        + (columns,) * 3
        + (depth, columns, depth),
        check_vma=False,
    )
```

time: 1240 us -> 617 us (0.50)
  waiting for transfers between devices: 885 us -> 348 us
  blocking collectives: 178 us -> 8.87 us
  starting transfers between devices: 1.46 us -> 75.9 us
  local copies, waits for them, and re-layouts: 17.9 us -> 58.1 us
  matrix products: 93.5 us -> 54.1 us
    all_gather x10 -> x2, waiting for transfers between devices: 326 us -> 50.3 us  [gather_pack(): own = lax.all_gather(pack, 'mp')]
    reduce_scatter x8 -> x2, waiting for transfers between devices: 320 us -> 54.9 us  [reduce_pack(): pack = lax.psum_scatter(pack, 'mp')]
    all_to_all x0 -> x12, waiting for transfers between devices: none -> 100 us  [the longest x9 79.1 us: exchange(): return lax.all_to_all(x, 'mp', 0, 0, tiled=True)]
    psum x2, waiting for transfers between devices: 237 us -> 139 us  [the longest x1 83.7 us: reduce_pack(): pack = lax.psum(pack, 'dp', axis_index_groups=COPIES)]
    all_gather x4 -> x0, blocking collectives: 94.5 us -> none  [the longest x2 45 us: merged(): gathered = jax.tree.map(lambda a: lax.all_gather(a, axis), part)]
    psum x2 -> x0, blocking collectives: 83.3 us -> none  [the longest x1 68.2 us: body(): lax.psum((grad_wq, grad_wk, grad_wv, grad_wout, gain_latent, gain_pixel,...]
    all_to_all x0 -> x12, starting transfers between devices: none -> 61.6 us  [the longest x9 38.6 us: exchange(): return lax.all_to_all(x, 'mp', 0, 0, tiled=True)]
    dot_general x48 -> x75, matrix products: 93.5 us -> 54.1 us  [the longest x50 36 us: dot(): lax.dot_general(a, b, (((1,), (0,)), ((), ())), preferred_element_type=f32)]
  transfers between devices with their start and end apart: 20 -> 27, of which waited for: 18 -> 18; matrix products, arithmetic and copies ran while one was open for 5% -> 19% of each run, Pallas kernels for 0% -> 0%
where the time goes in v1:
time: 617 us; the launch traced here: 607 us
  waiting for transfers between devices  348 us (56%)
  starting transfers between devices  75.9 us (12%)
  local copies, waits for them, and re-layouts  58.1 us (9%)
  matrix products  54.1 us (9%)
  other arithmetic  45 us (7%)
  between operations  17.3 us (3%)
  blocking collectives  8.87 us (1%)
    psum x1, waiting for transfers between devices, reduce_pack(): pack = lax.psum(pack, 'dp', axis_index_groups=COPIES)  83.7 us
    all_to_all x9, waiting for transfers between devices, exchange(): return lax.all_to_all(x, 'mp', 0, 0, tiled=True)  79.1 us
    psum x1, waiting for transfers between devices, body(): grad_qkv = lax.psum(jnp.stack(grad_qkv).astype(bf16), 'dp').astype(f32)  55.8 us
    reduce_scatter x2, waiting for transfers between devices, reduce_pack(): pack = lax.psum_scatter(pack, 'mp')  54.9 us
    all_gather x2, waiting for transfers between devices, gather_pack(): own = lax.all_gather(pack, 'mp')  50.3 us
    all_to_all x9, starting transfers between devices, exchange(): return lax.all_to_all(x, 'mp', 0, 0, tiled=True)  38.6 us
    dot_general x50, matrix products, dot(): lax.dot_general(a, b, (((1,), (0,)), ((), ())), preferred_element_type=f32)  36 us
    unnamed x337, local copies, waits for them, and re-layouts  21.8 us
  transfers between devices with their start and end apart: 27, of which 18 were waited for; matrix products, arithmetic and copies ran while one was open for 19% of the time, Pallas kernels for 0%

profile of v1, /device:TPU:1, one launch (start us, length us, event | category | flops | bytes accessed | tf_op | source)
XLA Modules:
  0.0 607.3 jit_solution(8202668595328506561)
XLA Ops:
  10.3 5.9 all-to-all-start
  19.3 7.8 %all-to-all-done = bf16[8,288,128]{2,1,0:T(8,128)(2,1)S(1)} async-done(((bf16[8,288,128]{2,1,0:T(8,128)(2,1)}), bf16[8,288,128]{2,1,0:T(8,128)(2,1)S(1)}, u32[]{:S(2)}, u32[]{:S(2)}) %all-to-all-start) | async-done | bytes 589856 | tf_op jit(solution)/shard_map/all_to_all | solution.py:54
  29.9 3.5 all-to-all-start.1
  35.4 12.2 %all-to-all-done.1 = bf16[8,288,128]{2,1,0:T(8,128)(2,1)S(1)} async-done(((bf16[8,288,128]{2,1,0:T(8,128)(2,1)}), bf16[8,288,128]{2,1,0:T(8,128)(2,1)S(1)}, u32[]{:S(2)}, u32[]{:S(2)}) %all-to-all-start.1) | async-done | bytes 589856 | tf_op jit(solution)/shard_map/all_to_all | solution.py:54
  53.7 5.5 all-to-all-start.2
  59.5 11.5 %all-to-all-done.2 = bf16[8,272,128]{2,1,0:T(8,128)(2,1)} async-done(((bf16[8,272,128]{2,1,0:T(8,128)(2,1)}), bf16[8,272,128]{2,1,0:T(8,128)(2,1)}, u32[]{:S(2)}, u32[]{:S(2)}) %all-to-all-start.2) | async-done | bytes 557088 | tf_op jit(solution)/shard_map/all_to_all | solution.py:54
  78.2 3.5 all-to-all-start.3
  82.7 9.6 %all-to-all-done.3 = bf16[8,272,128]{2,1,0:T(8,128)(2,1)S(1)} async-done(((bf16[8,272,128]{2,1,0:T(8,128)(2,1)}), bf16[8,272,128]{2,1,0:T(8,128)(2,1)S(1)}, u32[]{:S(2)}, u32[]{:S(2)}) %all-to-all-start.3) | async-done | bytes 557088 | tf_op jit(solution)/shard_map/all_to_all | solution.py:54
  102.6 3.6 all-to-all-start.4
  106.3 50.3 %all-gather.7.cloned.1.call-done = bf16[24,128,512]{2,1,0:T(8,128)(2,1)} async-done(((bf16[3,128,512]{2,1,0:T(8,128)(2,1)}), bf16[24,128,512]{2,1,0:T(8,128)(2,1)}) %all-gather.7.cloned.1.call-update) | async-done | bytes 3145744 | tf_op jit(solution)/shard_map/all_gather | solution.py:198
  158.6 3.6 fusion.191
  169.2 4.7 all-to-all-start.5
  176.6 4.9 all-to-all-done.5
  195.6 8.9 %all_to_all.65 = bf16[8,128,128]{2,1,0:T(8,128)(2,1)S(1)} all-to-all(bf16[8,128,128]{2,1,0:T(8,128)(2,1)S(1)} %bitcast.652), channel_id=1, replica_groups=mesh['dp'=16,'mp'=8] {'mp'}, dimensions={0} | all-to-all | bytes 524288 | tf_op jit(solution)/shard_map/all_to_all | solution.py:54
  213.3 3.7 all-to-all-start.7
  224.1 19.9 %all-to-all-done.7 = bf16[8,128,1024]{2,1,0:T(8,128)(2,1)S(1)} async-done(((bf16[8,128,1024]{2,1,0:T(8,128)(2,1)}), bf16[8,128,1024]{2,1,0:T(8,128)(2,1)S(1)}, u32[]{:S(2)}, u32[]{:S(2)}) %all-to-all-start.7) | async-done | bytes 2097184 | tf_op jit(solution)/shard_map/all_to_all | solution.py:54
  260.2 3.7 add_convert_fusion.1
  269.3 3.5 all-to-all-start.8
  275.5 8.1 %all-to-all-done.8 = bf16[8,272,128]{2,1,0:T(8,128)(2,1)S(1)} async-done(((bf16[8,272,128]{2,1,0:T(8,128)(2,1)}), bf16[8,272,128]{2,1,0:T(8,128)(2,1)S(1)}, u32[]{:S(2)}, u32[]{:S(2)}) %all-to-all-start.8) | async-done | bytes 557088 | tf_op jit(solution)/shard_map/all_to_all | solution.py:54
  294.1 3.5 add_convert_fusion
  307.0 4.6 all-to-all-start.9
  317.1 5.1 all-to-all-done.9
  329.0 3.4 all-to-all-start.12
  335.0 4.8 all-to-all-done.12
  339.9 8.3 %all-to-all-start.10 = ((bf16[64,40,128]{2,1,0:T(8,128)(2,1)}), bf16[64,40,128]{2,1,0:T(8,128)(2,1)}, u32[]{:S(2)}, u32[]{:S(2)}) async-start(bf16[64,40,128]{2,1,0:T(8,128)(2,1)} %bitcast.606), calls=%async_computation.10 | async-start | bytes 1310720 | tf_op jit(solution)/shard_map/all_to_all | solution.py:390
  349.1 55.8 %all-reduce.9.cloned.1.call-done = bf16[3,1024,128]{2,1,0:T(8,128)(2,1)} async-done(((bf16[3,1024,128]{2,1,0:T(8,128)(2,1)}), bf16[3,1024,128]{2,1,0:T(8,128)(2,1)}) %all-reduce.9.cloned.1.call-update) | async-done | bytes 786448 | tf_op jit(solution)/shard_map/psum | solution.py:439
  409.5 11.2 %all-to-all-start.11 = ((bf16[64,40,128]{2,1,0:T(8,128)(2,1)}), bf16[64,40,128]{2,1,0:T(8,128)(2,1)}, u32[]{:S(2)}, u32[]{:S(2)}) async-start(bf16[64,40,128]{2,1,0:T(8,128)(2,1)} %broadcast_in_dim.422), calls=%async_computation.11 | async-start | bytes 1310720 | tf_op jit(solution)/shard_map/all_to_all | solution.py:399
  425.2 16.3 %all-to-all-done.11 = bf16[64,40,128]{2,1,0:T(8,128)(2,1)} async-done(((bf16[64,40,128]{2,1,0:T(8,128)(2,1)}), bf16[64,40,128]{2,1,0:T(8,128)(2,1)}, u32[]{:S(2)}, u32[]{:S(2)}) %all-to-all-start.11) | async-done | bytes 655392 | tf_op jit(solution)/shard_map/all_to_all | solution.py:399
  445.2 6.9 %reduce-scatter.3.cloned.1.call-done = bf16[1,2,128,512]{3,2,1,0:T(8,128)(2,1)} async-done(((bf16[8,2,128,512]{3,2,1,0:T(8,128)(2,1)}), bf16[1,2,128,512]{3,2,1,0:T(8,128)(2,1)}) %reduce-scatter.3.cloned.1.call-update) | async-done | bytes 262160 | tf_op jit(solution)/shard_map/reduce_scatter | solution.py:428
  452.2 48.0 %reduce-scatter.5.cloned.1.call-done = bf16[1,3,128,512]{3,2,1,0:T(8,128)(2,1)} async-done(((bf16[8,3,128,512]{3,2,1,0:T(8,128)(2,1)}), bf16[1,3,128,512]{3,2,1,0:T(8,128)(2,1)}) %reduce-scatter.5.cloned.1.call-update) | async-done | bytes 393232 | tf_op jit(solution)/shard_map/reduce_scatter | solution.py:428
  504.1 83.7 %all-reduce.11.cloned.1.call-done = (bf16[2,128,512]{2,1,0:T(8,128)(2,1)}, bf16[3,128,512]{2,1,0:T(8,128)(2,1)}) async-done(((bf16[2,128,512]{2,1,0:T(8,128)(2,1)}, bf16[3,128,512]{2,1,0:T(8,128)(2,1)}), (bf16[2,128,512]{2,1,0:T(8,128)(2,1)}, bf16[3,128,512]{2,1,0:T(8,128)(2,1)})) %all-reduce.11.cloned.1.call-update) | async-done | bytes 655376 | tf_op jit(solution)/shard_map/psum | solution.py:429
  587.7 5.7 collective-permute-start.6
  (607 shorter events, 158.2 us)
Async XLA Ops:
  7.2 156.9 %copy-start = (bf16[1024,128]{1,0:T(8,128)(2,1)S(1)}, bf16[1024,128]{1,0:T(8,128)(2,1)}, u32[]{:S(2)}) copy-start(bf16[1024,128]{1,0:T(8,128)(2,1)} %param.36) | copy-start | bytes 786436
  10.3 16.8 %all-to-all-start = ((bf16[8,288,128]{2,1,0:T(8,128)(2,1)}), bf16[8,288,128]{2,1,0:T(8,128)(2,1)S(1)}, u32[]{:S(2)}, u32[]{:S(2)}) async-start(bf16[8,288,128]{2,1,0:T(8,128)(2,1)} %pad_maximum_fusion.5), calls=%async_computation | async-start | bytes 1179648 | tf_op jit(solution)/shard_map/all_to_all | solution.py:54
  16.2 76.2 %all-gather.5.cloned.1.call-start = ((), (), s32[]{:S(2)}) async-start(), calls=%async_computation.18 | async-start | bytes 2359296 | tf_op jit(solution)/shard_map/all_gather | solution.py:198
  29.9 17.7 %all-to-all-start.1 = ((bf16[8,288,128]{2,1,0:T(8,128)(2,1)}), bf16[8,288,128]{2,1,0:T(8,128)(2,1)S(1)}, u32[]{:S(2)}, u32[]{:S(2)}) async-start(bf16[8,288,128]{2,1,0:T(8,128)(2,1)} %broadcast_in_dim.378), calls=%async_computation.1 | async-start | bytes 1179648 | tf_op jit(solution)/shard_map/all_to_all | solution.py:54
  48.3 3.2 collective-permute-start
  49.4 44.9 %copy-start.128 = (pred[272]{0:T(512)(128)(4,1)}, pred[272]{0:T(512)(128)(4,1)S(1)}, u32[]{:S(2)}) copy-start(pred[272]{0:T(512)(128)(4,1)S(1)} %iota_compare_fusion.8) | copy-start | bytes 820
  53.7 17.3 %all-to-all-start.2 = ((bf16[8,272,128]{2,1,0:T(8,128)(2,1)}), bf16[8,272,128]{2,1,0:T(8,128)(2,1)}, u32[]{:S(2)}, u32[]{:S(2)}) async-start(bf16[8,272,128]{2,1,0:T(8,128)(2,1)} %broadcast_in_dim.382), calls=%async_computation.2 | async-start | bytes 1114112 | tf_op jit(solution)/shard_map/all_to_all | solution.py:54
  78.2 14.1 %all-to-all-start.3 = ((bf16[8,272,128]{2,1,0:T(8,128)(2,1)}), bf16[8,272,128]{2,1,0:T(8,128)(2,1)S(1)}, u32[]{:S(2)}, u32[]{:S(2)}) async-start(bf16[8,272,128]{2,1,0:T(8,128)(2,1)} %copy.181), calls=%async_computation.3 | async-start | bytes 1114112 | tf_op jit(solution)/shard_map/all_to_all | solution.py:54
  81.8 74.8 %all-gather.7.cloned.1.call-start = ((), (), s32[]{:S(2)}) async-start(), calls=%async_computation.19 | async-start | bytes 3538944 | tf_op jit(solution)/shard_map/all_gather | solution.py:198
  92.4 5.4 collective-permute-start.1
  102.6 59.6 %all-to-all-start.4 = ((bf16[8,128,1024]{2,1,0:T(8,128)(2,1)}), bf16[8,128,1024]{2,1,0:T(8,128)(2,1)S(1)}, u32[]{:S(2)}, u32[]{:S(2)}) async-start(bf16[8,128,1024]{2,1,0:T(8,128)(2,1)} %broadcast_in_dim.403), calls=%async_computation.4 | async-start | bytes 4194304 | tf_op jit(solution)/shard_map/all_to_all | solution.py:54
  156.5 28.4 %collective-permute-start.2 = (bf16[8,3,128,512]{3,2,1,0:T(8,128)(2,1)}, bf16[8,3,128,512]{3,2,1,0:T(8,128)(2,1)}, u32[]{:S(2)}, u32[]{:S(2)}) collective-permute-start(bf16[8,3,128,512]{3,2,1,0:T(8,128)(2,1)} %bitcast.600), channel_id=1, source_target_pairs={{0,8},{8,0},{16,24},{24,16},{32,40},{40,32},{48,56},{56,48},{64,72... | collective-permute-start | bytes 9437192 | tf_op jit(solution)/shard_map/ppermute | solution.py:50
  169.2 12.2 %all-to-all-start.5 = ((bf16[8,128,128]{2,1,0:T(8,128)(2,1)}), bf16[8,128,128]{2,1,0:T(8,128)(2,1)}, u32[]{:S(2)}, u32[]{:S(2)}) async-start(bf16[8,128,128]{2,1,0:T(8,128)(2,1)} %bitcast.650), calls=%async_computation.5 | async-start | bytes 524288 | tf_op jit(solution)/shard_map/all_to_all | solution.py:54
  213.3 30.7 %all-to-all-start.7 = ((bf16[8,128,1024]{2,1,0:T(8,128)(2,1)}), bf16[8,128,1024]{2,1,0:T(8,128)(2,1)S(1)}, u32[]{:S(2)}, u32[]{:S(2)}) async-start(bf16[8,128,1024]{2,1,0:T(8,128)(2,1)} %bitcast.567), calls=%async_computation.7 | async-start | bytes 4194304 | tf_op jit(solution)/shard_map/all_to_all | solution.py:54
  217.0 187.8 %all-reduce.9.cloned.1.call-start = ((), (), s32[]{:S(2)}) async-start(), calls=%async_computation.16 | async-start | bytes 1572864 | tf_op jit(solution)/shard_map/psum | solution.py:439
  222.1 70.7 %collective-permute-start.7 = (bf16[8,3,128,512]{3,2,1,0:T(8,128)(2,1)}, bf16[8,3,128,512]{3,2,1,0:T(8,128)(2,1)}, u32[]{:S(2)}, u32[]{:S(2)}) collective-permute-start(bf16[8,3,128,512]{3,2,1,0:T(8,128)(2,1)} %pad_maximum_fusion), channel_id=1, source_target_pairs={{0,8},{8,0},{16,24},{24,16},{32,40},{40,32},{48,56},{56,48},{64,72... | collective-permute-start | bytes 9437192 | tf_op jit(solution)/shard_map/ppermute | solution.py:50
  251.1 9.2 %collective-permute-start.5 = (bf16[8,2,128,512]{3,2,1,0:T(8,128)(2,1)}, bf16[8,2,128,512]{3,2,1,0:T(8,128)(2,1)}, u32[]{:S(2)}, u32[]{:S(2)}) collective-permute-start(bf16[8,2,128,512]{3,2,1,0:T(8,128)(2,1)} %pad_maximum_fusion.1), channel_id=1, source_target_pairs={{0,8},{8,0},{16,24},{24,16},{32,40},{40,32},{48,56},{56,48},{64,72... | collective-permute-start | bytes 6291464 | tf_op jit(solution)/shard_map/ppermute | solution.py:50
  258.7 193.5 %reduce-scatter.3.cloned.1.call-start = ((), (), s32[]{:S(2)}) async-start(), calls=%async_computation.15 | async-start | bytes 2359296 | tf_op jit(solution)/shard_map/reduce_scatter | solution.py:428
  269.3 14.3 %all-to-all-start.8 = ((bf16[8,272,128]{2,1,0:T(8,128)(2,1)}), bf16[8,272,128]{2,1,0:T(8,128)(2,1)S(1)}, u32[]{:S(2)}, u32[]{:S(2)}) async-start(bf16[8,272,128]{2,1,0:T(8,128)(2,1)} %broadcast_in_dim.416), calls=%async_computation.8 | async-start | bytes 1114112 | tf_op jit(solution)/shard_map/all_to_all | solution.py:54
  272.9 227.3 %reduce-scatter.5.cloned.1.call-start = ((), (), s32[]{:S(2)}) async-start(), calls=%async_computation.17 | async-start | bytes 3538944 | tf_op jit(solution)/shard_map/reduce_scatter | solution.py:428
  307.0 15.2 %all-to-all-start.9 = ((bf16[8,272,128]{2,1,0:T(8,128)(2,1)}), bf16[8,272,128]{2,1,0:T(8,128)(2,1)}, u32[]{:S(2)}, u32[]{:S(2)}) async-start(bf16[8,272,128]{2,1,0:T(8,128)(2,1)} %copy.200), calls=%async_computation.9 | async-start | bytes 1114112 | tf_op jit(solution)/shard_map/all_to_all | solution.py:54
  328.2 4.2 collective-permute-start.3
  329.0 10.9 %all-to-all-start.12 = ((bf16[8,128,128]{2,1,0:T(8,128)(2,1)}), bf16[8,128,128]{2,1,0:T(8,128)(2,1)S(1)}, u32[]{:S(2)}, u32[]{:S(2)}) async-start(bf16[8,128,128]{2,1,0:T(8,128)(2,1)} %bitcast.130), calls=%async_computation.12 | async-start | bytes 524288 | tf_op jit(solution)/shard_map/all_to_all | solution.py:414
  339.9 67.4 %all-to-all-start.10 = ((bf16[64,40,128]{2,1,0:T(8,128)(2,1)}), bf16[64,40,128]{2,1,0:T(8,128)(2,1)}, u32[]{:S(2)}, u32[]{:S(2)}) async-start(bf16[64,40,128]{2,1,0:T(8,128)(2,1)} %bitcast.606), calls=%async_computation.10 | async-start | bytes 1310720 | tf_op jit(solution)/shard_map/all_to_all | solution.py:390
  409.5 32.0 %all-to-all-start.11 = ((bf16[64,40,128]{2,1,0:T(8,128)(2,1)}), bf16[64,40,128]{2,1,0:T(8,128)(2,1)}, u32[]{:S(2)}, u32[]{:S(2)}) async-start(bf16[64,40,128]{2,1,0:T(8,128)(2,1)} %broadcast_in_dim.422), calls=%async_computation.11 | async-start | bytes 1310720 | tf_op jit(solution)/shard_map/all_to_all | solution.py:399
  420.7 167.0 %all-reduce.11.cloned.1.call-start = ((), (), s32[]{:S(2)}) async-start(), calls=%async_computation.20 | async-start | bytes 1310720 | tf_op jit(solution)/shard_map/psum | solution.py:429
  442.9 2.2 collective-permute-start.4
  445.2 55.7 %copy-start.97 = (bf16[144,1024]{1,0:T(8,128)(2,1)S(1)}, bf16[144,1024]{1,0:T(8,128)(2,1)}, u32[]{:S(2)}) copy-start(bf16[144,1024]{1,0:T(8,128)(2,1)} %get-tuple-element.175) | copy-start | bytes 884740
  445.2 55.7 %copy-start.98 = (bf16[144,1024]{1,0:T(8,128)(2,1)S(1)}, bf16[144,1024]{1,0:T(8,128)(2,1)}, u32[]{:S(2)}) copy-start(bf16[144,1024]{1,0:T(8,128)(2,1)} %get-tuple-element.176) | copy-start | bytes 884740
  500.9 93.1 %copy-start.111 = (bf16[261,128]{1,0:T(8,128)(2,1)S(1)}, bf16[261,128]{1,0:T(8,128)(2,1)}, u32[]{:S(2)}) copy-start(bf16[261,128]{1,0:T(8,128)(2,1)} %param.31) | copy-start | bytes 200452
  587.7 7.5 %collective-permute-start.6 = (bf16[2,128,512]{2,1,0:T(8,128)(2,1)}, bf16[2,128,512]{2,1,0:T(8,128)(2,1)S(1)}, u32[]{:S(2)}, u32[]{:S(2)}) collective-permute-start(bf16[2,128,512]{2,1,0:T(8,128)(2,1)} %get-tuple-element.139), channel_id=1, source_target_pairs={{0,8},{8,0},{16,24},{24,16},{32,40},{40,32},{48,56},{56,48},{64,72... | collective-permute-start | bytes 786440 | tf_op jit(solution)/shard_map/ppermute | solution.py:50
  595.2 2.0 collective-permute-start.8
  (158 other events, 691.0 us)
Sparse Core Ops, SparseCore 0:
  19.2 44.7 all-gather.4
  84.8 71.6 all-gather.6
  258.8 146.0 all-reduce.8
  407.3 44.8 reduce-scatter.2
  454.6 45.5 reduce-scatter.4
  502.7 84.9 all-reduce.10
